TPU v7x, 128 devices: a whole 4x4x4 slice. The times are simulated.
128 devices in a mesh: dp: 16 (over z, y), tensor: 8 (over x, core).
Axes of the slice: x: 4, y: 4, z: 4, core: 2. Of those that a mesh axis runs over, the one named last changes fastest.
Arguments:
- grad_query: bfloat16 [16, 1, 4096, 4608], P('dp', None, 'tensor'), may hold values from -33 to 33
- grad_key: bfloat16 [16, 1, 2048, 4608], P('dp', None, 'tensor'), may hold values from -33 to 33
- error_query: bfloat16 [16, 1, 4096, 4608], P('dp', None, 'tensor'), may hold values from -12 to 12
- error_key: bfloat16 [16, 1, 2048, 4608], P('dp', None, 'tensor'), may hold values from -12 to 12
- factor_query: bfloat16 [1, 4608, 64], replicated, may hold values from -0.09375 to 0.09375
- factor_key: bfloat16 [1, 4608, 64], replicated, may hold values from -0.09375 to 0.09375
Outputs:
- error_query_new: bfloat16 [16, 1, 4096, 4608], P('dp', None, 'tensor')
- error_key_new: bfloat16 [16, 1, 2048, 4608], P('dp', None, 'tensor')
- factor_query_new: bfloat16 [1, 4608, 64], replicated
- factor_key_new: bfloat16 [1, 4608, 64], replicated
All inputs are finite; a program needn't handle non-finite values.
Results may differ from a plain program's by a relative error of at most 0.0085.
Values may be sent and summed in bfloat16 or wider, within the bound.
A program may use at most 128 MiB of HBM per device.

v0:
```python
import jax
import jax.numpy as jnp
from jax import lax
from jax.sharding import PartitionSpec as P


def merged_rows(grad, error):
    return (grad[0].astype(jnp.float32) + error[0].astype(jnp.float32)).astype(jnp.bfloat16)


def images(merged, factor):
    return jnp.einsum("lhd,ldr->lhr", merged, factor, preferred_element_type=jnp.float32)


def gram_of(field):
    return jnp.einsum("lhr,lhs->lrs", field, field, precision=lax.Precision.HIGHEST)


def orthonormal(field, gram):
    lower = jnp.linalg.cholesky(gram)
    solved = jax.scipy.linalg.solve_triangular(lower, jnp.swapaxes(field, 1, 2), lower=True)
    return jnp.swapaxes(solved, 1, 2).astype(jnp.bfloat16)


def projected(merged, basis):
    return jnp.einsum("lhd,lhr->ldr", merged, basis, preferred_element_type=jnp.float32)


def body(grad_query, grad_key, error_query, error_key, factor_query, factor_key):
    replicas = lax.axis_size("dp")
    merged_q = merged_rows(grad_query, error_query)
    merged_k = merged_rows(grad_key, error_key)
    image_q = images(merged_q, factor_query)
    image_k = images(merged_k, factor_key)
    image_q, image_k = lax.psum((image_q, image_k), "dp")
    gram_q, gram_k = lax.psum((gram_of(image_q), gram_of(image_k)), "tensor")
    basis_q = orthonormal(image_q, gram_q)
    basis_k = orthonormal(image_k, gram_k)
    summed_q, summed_k = lax.psum(
        (projected(merged_q, basis_q), projected(merged_k, basis_k)), ("dp", "tensor")
    )
    new_q = summed_q.astype(jnp.bfloat16)
    new_k = summed_k.astype(jnp.bfloat16)

    def refresh(merged, basis, factor):
        approx = jnp.einsum("lhr,ldr->lhd", basis, factor, preferred_element_type=jnp.float32)
        return (merged.astype(jnp.float32) - approx / replicas).astype(jnp.bfloat16)[None]

    return (refresh(merged_q, basis_q, new_q), refresh(merged_k, basis_k, new_k), new_q, new_k)


def solution(mesh):
    placed = (
        P("dp", None, "tensor", None),
        P("dp", None, "tensor", None),
        P("dp", None, "tensor", None),
        P("dp", None, "tensor", None),
        P(),
        P(),
    )
    return jax.shard_map(
        body,
        mesh=mesh,
        in_specs=placed,
        out_specs=(P("dp", None, "tensor", None), P("dp", None, "tensor", None), P(), P()),
        check_vma=False,
    )
```

profile of v0, /device:TPU:1, one launch (start us, length us, event | category | flops | bytes accessed | tf_op | source)
XLA Modules:
  0.0 279.4 jit_solution(16911609590611879887)
XLA Ops:
  7.2 0.0 copy-start
  7.2 0.0 copy-start.1
  7.2 0.0 copy-start.4
  7.2 0.0 all-reduce.6.cloned.1.call-start
  7.2 1.0 copy-done
  8.2 0.0 copy-start.2
  8.2 6.1 %convolution_bitcast_fusion.2 = f32[1,512,64]{1,2,0:T(8,128)} fusion(bf16[1,4608,64]{1,2,0:T(8,128)(2,1)S(1)} %copy-done, bf16[1,1,512,4608]{3,2,1,0:T(8,128)(2,1)} %param.9, bf16[1,1,512,4608]{3,2,1,0:T(8,128)(2,1)} %param.7), kind=kOutput, calls=%fused_computation.12 | convolution fusion | flops 311427072 | bytes 10158080 | tf_op jit(solution)/shard_map/lhd,ldr->lhr/dot_general | solution.py:12
  14.4 0.0 copy-done.1
  14.4 0.0 copy-done.4
  14.4 0.0 copy-done.2
  14.4 1.5 convolution_bitcast_fusion.3
  15.9 0.0 all-reduce.6.cloned.1.call-update
  15.9 85.8 %all-reduce.6.cloned.1.call-done = (f32[1,512,64]{1,2,0:T(8,128)}, f32[1,256,64]{1,2,0:T(8,128)}) async-done(((f32[1,512,64]{1,2,0:T(8,128)}, f32[1,256,64]{1,2,0:T(8,128)}), (f32[1,512,64]{1,2,0:T(8,128)}, f32[1,256,64]{1,2,0:T(8,128)})) %all-reduce.6.cloned.1.call-update) | async-done | bytes 196624 | tf_op jit(solution)/shard_map/psum | solution.py:35
  101.7 0.0 copy-start.6
  101.7 1.1 convolution_bitcast_fusion.4
  102.8 1.2 convolution_bitcast_fusion.5
  104.1 23.1 %all-reduce.2 = (f32[1,64,64]{1,2,0:T(8,128)S(1)}, f32[1,64,64]{1,2,0:T(8,128)S(1)}) all-reduce(f32[1,64,64]{1,2,0:T(8,128)S(1)} %convolution_bitcast_fusion.5, f32[1,64,64]{1,2,0:T(8,128)S(1)} %convolution_bitcast_fusion.4), channel_id=1, replica_groups=mesh['dp'=16,'tensor'=8] {'tensor'}, use_global_device_ids=true, to_apply=%region_1.0 | all-reduce | flops 8192 | bytes 65536 | tf_op jit(solution)/shard_map/psum | solution.py:36
  127.2 0.1 copy.11
  127.3 0.1 copy.13
  127.4 5.8 %custom-call.15 = f32[1,64,64]{2,1,0:T(8,128)S(1)} custom-call(f32[1,64,64]{2,1,0:T(8,128)S(1)} %get-tuple-element.11), custom_call_target="Cholesky" | custom-call | tf_op jit(solution)/shard_map/jit(cholesky)/cholesky | solution.py:20
  133.3 0.6 compare_reduce_fusion
  133.9 0.7 select_select_fusion
  134.6 4.9 %custom-call.12 = f32[1,64,64]{1,2,0:T(8,128)S(1)} custom-call(f32[1,64,64]{2,1,0:T(8,128)S(1)} %select_select_fusion), custom_call_target="InvertDiagBlocksLowerTriangular" | custom-call | tf_op jit(solution)/shard_map/jit(_solve_triangular)/triangular_solve | solution.py:21
  139.5 1.1 fusion.7
  140.6 3.4 %convolution_bitcast_fusion = f32[1,4608,64]{1,2,0:T(8,128)} fusion(bf16[256,64]{0,1:T(8,128)(2,1)S(1)} %fusion.7, bf16[1,1,256,4608]{3,2,1,0:T(8,128)(2,1)S(1)} %copy-done.1, bf16[1,1,256,4608]{3,2,1,0:T(8,128)(2,1)} %param.8), kind=kOutput, calls=%fused_computation.7 | convolution fusion | flops 155713536 | bytes 5931008 | tf_op jit(solution)/shard_map/lhd,lhr->ldr/dot_general | solution.py:26
  144.0 5.8 %custom-call.14 = f32[1,64,64]{2,1,0:T(8,128)S(1)} custom-call(f32[1,64,64]{2,1,0:T(8,128)S(1)} %get-tuple-element.12), custom_call_target="Cholesky" | custom-call | tf_op jit(solution)/shard_map/jit(cholesky)/cholesky | solution.py:20
  149.9 0.6 compare_reduce_fusion.1
  150.6 0.7 select_select_fusion.1
  151.2 4.9 %custom-call.11 = f32[1,64,64]{1,2,0:T(8,128)S(1)} custom-call(f32[1,64,64]{2,1,0:T(8,128)S(1)} %select_select_fusion.1), custom_call_target="InvertDiagBlocksLowerTriangular" | custom-call | tf_op jit(solution)/shard_map/jit(_solve_triangular)/triangular_solve | solution.py:21
  156.1 0.0 copy-done.6
  156.1 0.3 fusion.6
  156.5 6.2 %convolution_bitcast_fusion.1 = f32[1,4608,64]{1,2,0:T(8,128)} fusion(bf16[512,64]{0,1:T(8,128)(2,1)S(1)} %fusion.6, bf16[1,1,512,4608]{3,2,1,0:T(8,128)(2,1)} %param.9, bf16[1,1,512,4608]{3,2,1,0:T(8,128)(2,1)} %param.7), kind=kOutput, calls=%fused_computation.8 | convolution fusion | flops 311427072 | bytes 10682368 | tf_op jit(solution)/shard_map/lhd,lhr->ldr/dot_general | solution.py:26
  162.7 99.2 %all-reduce.7 = (bf16[1,4608,64]{1,2,0:T(8,128)(2,1)}, bf16[1,4608,64]{1,2,0:T(8,128)(2,1)}) all-reduce(f32[1,4608,64]{1,2,0:T(8,128)} %convolution_bitcast_fusion.1, f32[1,4608,64]{1,2,0:T(8,128)} %convolution_bitcast_fusion), channel_id=1, replica_groups=mesh['dp'=16,'tensor'=8] {'dp','tensor'}, use_global_device_ids=true, to_apply=%region_4.6 | all-reduce | flops 589824 | bytes 3538944 | tf_op jit(solution)/shard_map/psum | solution.py:39
  261.9 0.0 copy-start.3
  261.9 0.0 copy-start.5
  261.9 8.2 %fusion.1 = bf16[1,1,512,4608]{3,2,1,0:T(8,128)(2,1)} fusion(bf16[512,64]{0,1:T(8,128)(2,1)S(1)} %fusion.6, bf16[1,4608,64]{1,2,0:T(8,128)(2,1)} %get-tuple-element.5, bf16[1,1,512,4608]{3,2,1,0:T(8,128)(2,1)} %param.9, bf16[1,1,512,4608]{3,2,1,0:T(8,128)(2,1)} %param.7), kind=kOutput, calls=%fused_computation.4 | convolution fusion | flops 320864256 | bytes 14811136 | tf_op jit(solution)/shard_map/lhr,ldr->lhd/dot_general | solution.py:46
  270.1 0.0 copy-done.3
  270.1 0.0 copy-done.5
  270.1 2.4 fusion.3
  (3 shorter events, 0.1 us)
Async XLA Ops:
  7.2 1.1 copy-start
  7.2 7.2 %copy-start.1 = (bf16[1,1,256,4608]{3,2,1,0:T(8,128)(2,1)S(1)}, bf16[1,1,256,4608]{3,2,1,0:T(8,128)(2,1)}, u32[]{:S(2)}) copy-start(bf16[1,1,256,4608]{3,2,1,0:T(8,128)(2,1)} %param.10) | copy-start | bytes 7077892
  7.2 7.2 %copy-start.4 = (bf16[1,4608,64]{1,2,0:T(8,128)(2,1)S(1)}, bf16[1,4608,64]{1,2,0:T(8,128)(2,1)}, u32[]{:S(2)}) copy-start(bf16[1,4608,64]{1,2,0:T(8,128)(2,1)} %param.12) | copy-start | bytes 1769476
  7.2 94.5 %all-reduce.6.cloned.1.call-start = ((), (), s32[]{:S(2)}) async-start(), calls=%async_computation | async-start | bytes 393216 | tf_op jit(solution)/shard_map/psum | solution.py:35
  8.2 6.1 %copy-start.2 = (bf16[1,1,256,4608]{3,2,1,0:T(8,128)(2,1)S(1)}, bf16[1,1,256,4608]{3,2,1,0:T(8,128)(2,1)}, u32[]{:S(2)}) copy-start(bf16[1,1,256,4608]{3,2,1,0:T(8,128)(2,1)} %param.8) | copy-start | bytes 7077892
  101.7 54.4 %copy-start.6 = (f32[1,512,64]{1,2,0:T(8,128)S(1)}, f32[1,512,64]{1,2,0:T(8,128)}, u32[]{:S(2)}) copy-start(f32[1,512,64]{1,2,0:T(8,128)} %get-tuple-element.7) | copy-start | bytes 393220
  261.9 8.2 %copy-start.3 = (bf16[1,1,256,4608]{3,2,1,0:T(8,128)(2,1)S(1)}, bf16[1,1,256,4608]{3,2,1,0:T(8,128)(2,1)}, u32[]{:S(2)}) copy-start(bf16[1,1,256,4608]{3,2,1,0:T(8,128)(2,1)} %param.8) | copy-start | bytes 7077892
  261.9 8.2 %copy-start.5 = (bf16[1,4608,64]{1,2,0:T(8,128)(2,1)S(1)}, bf16[1,4608,64]{1,2,0:T(8,128)(2,1)}, u32[]{:S(2)}) copy-start(bf16[1,4608,64]{1,2,0:T(8,128)(2,1)} %get-tuple-element.6) | copy-start | bytes 1769476
Sparse Core Ops, SparseCore 0:
  16.0 85.6 all-reduce.5
where the time goes:
time: 281 us; the launch traced here: 279 us
  blocking collectives  122 us (43%)
  waiting for transfers between devices  85.8 us (31%)
  matrix products  31.7 us (11%)
  other arithmetic  24.2 us (9%)
  between operations  14.1 us (5%)
    psum x1, blocking collectives, body(): lax.psum((projected(merged_q, basis_q), projected(merged_k, basis_k)), ('...  99.2 us
    psum x1, waiting for transfers between devices, body(): image_q, image_k = lax.psum((image_q, image_k), 'dp')  85.8 us
    psum x1, blocking collectives, body(): gram_q, gram_k = lax.psum((gram_of(image_q), gram_of(image_k)), 'tensor')  23.1 us
    another operation x6, other arithmetic, orthonormal(): lower = jnp.linalg.cholesky(gram)  13 us
    another operation x4, other arithmetic, orthonormal(): jax.scipy.linalg.solve_triangular(lower, jnp.swapaxes(field, 1, 2), lower...  11.1 us
    dot_general x2, matrix products, refresh(): jnp.einsum('lhr,ldr->lhd', basis, factor, preferred_element_type=jnp.floa...  10.7 us
    dot_general x2, matrix products, projected(): jnp.einsum('lhd,lhr->ldr', merged, basis, preferred_element_type=jnp.floa...  9.64 us
    dot_general x2, matrix products, images(): jnp.einsum('lhd,ldr->lhr', merged, factor, preferred_element_type=jnp.flo...  7.62 us
  transfers between devices with their start and end apart: 1, of which 1 were waited for; matrix products, arithmetic and copies ran while one was open for 0% of the time, Pallas kernels for 0%

commit v1 on v0

v1 whole, which is shorter than its diff:
```python
import jax
import jax.numpy as jnp
from jax import lax
from jax.experimental import pallas as pl
from jax.experimental.pallas import tpu as pltpu
from jax.sharding import PartitionSpec as P

F32, BF16 = jnp.float32, jnp.bfloat16
D, RANK = 4608, 64
RQ, RK = 512, 256
ROWS = RQ + RK
CHUNK = 768
CHUNKS = D // CHUNK
HALF = D // 2
PART = HALF // 3
LANES = PART // 2
MESH = pl.DeviceIdType.MESH


def dot(a, b, ca=1, cb=0, precision=None):
    return lax.dot_general(a, b, (((ca,), (cb,)), ((), ())), precision=precision, preferred_element_type=F32)


def at(start, size, unit):
    return pl.ds(pl.multiple_of(start, unit), size)


def factorize(gram, inv_ref):
    lane = lax.broadcasted_iota(jnp.int32, (8, 128), 1)
    row = lax.broadcasted_iota(jnp.int32, (8, 128), 0)
    side = jnp.where(lane >= RANK, RANK, 0)
    g = [gram[8 * i:8 * i + 8, :] for i in range(8)]
    w = [jnp.where(lane - side == row + 8 * i, 1.0, 0.0).astype(F32) for i in range(8)]

    def column(x, j):
        return jnp.take_along_axis(x, side + j, axis=1, mode="promise_in_bounds")

    for j in range(RANK):
        b, t = divmod(j, 8)
        row_g = jnp.broadcast_to(g[b][t:t + 1, :], (8, 128))
        row_w = jnp.broadcast_to(w[b][t:t + 1, :], (8, 128))
        pivot = column(row_g, j)
        inverse = 1.0 / pivot
        inv_ref[j:j + 1, :] = (row_w * lax.rsqrt(pivot))[0:1, :]
        scaled_g, scaled_w = row_g * inverse, row_w * inverse
        for i in range(b, 8):
            c = column(g[i], j)
            if i == b:
                c = jnp.where(row > t, c, 0.0)
            g[i] = g[i] - c * scaled_g
            w[i] = w[i] - c * scaled_w


def reduce_kernel(gq, gk, eq, ek, fq, fk, merged, basis, psum, inv,
                  ebuf, fbuf, acc, ar1, ar2, packed, image_t, image_h,
                  gsend, gsib, gx, psend, psib, pown, rs, ar3,
                  lsem, fsem, s_ar1, r_ar1, s_ar2, r_ar2, s_g, r_g, s_gx, r_gx,
                  s_p, r_p, s_rs, r_rs, s_a3, r_a3, s_ag, r_ag, s_fw, r_fw):
    dp, tensor = lax.axis_index("dp"), lax.axis_index("tensor")
    z, y = lax.div(dp, 4), lax.rem(dp, 4)
    x, c = lax.div(tensor, 2), lax.rem(tensor, 2)

    def device(dz=0, dy=0, dx=0, dc=0):
        return (lax.rem(z + dz, 4) * 4 + lax.rem(y + dy, 4), lax.rem(x + dx, 4) * 2 + lax.rem(c + dc, 2))

    def send(src, dst, ssem, rsem, to):
        pltpu.make_async_remote_copy(src, dst, ssem, rsem, device_id=to, device_id_type=MESH).start()

    def arrived(ref, rsem, ssem):
        pltpu.make_async_remote_copy(ref, ref, ssem, rsem, device_id=device(dc=1), device_id_type=MESH).wait_recv()

    def sent(ref, rsem, ssem):
        pltpu.make_async_remote_copy(ref, ref, ssem, rsem, device_id=device(dc=1), device_id_type=MESH).wait_send()

    loads = [
        pltpu.make_async_copy(fq.at[0], fbuf.at[0], fsem),
        pltpu.make_async_copy(fk.at[0], fbuf.at[1], fsem),
    ]
    for cp in loads:
        cp.start()

    def load(k):
        cols = at(k * CHUNK, CHUNK, 128)
        return [
            pltpu.make_async_copy(gq.at[0, 0, :, cols], merged.at[0:RQ, cols], lsem.at[k]),
            pltpu.make_async_copy(eq.at[0, 0, :, cols], ebuf.at[0:RQ, cols], lsem.at[k]),
            pltpu.make_async_copy(gk.at[0, 0, :, cols], merged.at[RQ:ROWS, cols], lsem.at[k]),
            pltpu.make_async_copy(ek.at[0, 0, :, cols], ebuf.at[RQ:ROWS, cols], lsem.at[k]),
        ]

    for k in range(CHUNKS):
        for cp in load(k):
            cp.start()

    offsets = [(a, b, d) for a in range(4) for b in range(4) for d in range(4) if (a, b, d) != (0, 0, 0) and 0 in (a, b, d)]
    barrier = pltpu.get_barrier_semaphore()
    peers = [device(a, b, d) for a, b, d in offsets] + [device(dc=1)]
    for to in peers:
        pl.semaphore_signal(barrier, 1, device_id=to, device_id_type=MESH)

    acc[...] = jnp.zeros_like(acc)
    for cp in loads:
        cp.wait()

    def merge(k, carry):
        cols = at(k * CHUNK, CHUNK, 128)
        for cp in load(k):
            cp.wait()
        for block in range(3):
            rows = slice(256 * block, 256 * block + 256)
            m = (merged[rows, cols].astype(F32) + ebuf[rows, cols].astype(F32)).astype(BF16)
            merged[rows, cols] = m
            acc[rows, :] += dot(m, fbuf[block // 2, :, cols], 1, 1)
        return carry

    lax.fori_loop(0, CHUNKS, merge, 0)

    halves = (ar1.at[0, z], ar1.at[1, y])
    top = jnp.concatenate([acc[0:256, :], acc[256:512, :]], axis=1).astype(BF16)
    low = jnp.concatenate([acc[512:640, :], acc[640:768, :]], axis=1).astype(BF16)
    halves[0][...] = top[0:192]
    halves[1][0:64, :] = top[192:256]
    halves[1][64:192, :] = low
    pl.semaphore_wait(barrier, len(peers))
    for d in (1, 2, 3):
        send(ar1.at[0, z], ar1.at[0, z], s_ar1.at[0], r_ar1.at[0], device(dz=d))
        send(ar1.at[1, y], ar1.at[1, y], s_ar1.at[1], r_ar1.at[1], device(dy=d))
    for h, mine in ((0, y), (1, z)):
        arrived(ar1.at[h, 0:3], r_ar1.at[h], s_ar1.at[h])
        total = ar1[h, 0].astype(F32)
        for s in (1, 2, 3):
            total += ar1[h, s].astype(F32)
        ar2[h, mine] = total.astype(BF16)
        for d in (1, 2, 3):
            to = device(dy=d) if h == 0 else device(dz=d)
            send(ar2.at[h, mine], ar2.at[h, mine], s_ar2.at[h], r_ar2.at[h], to)
    for h in (0, 1):
        arrived(ar2.at[h, 0:3], r_ar2.at[h], s_ar2.at[h])
        total = ar2[h, 0].astype(F32)
        for s in (1, 2, 3):
            total += ar2[h, s].astype(F32)
        packed[192 * h:192 * h + 192, :] = total

    flipped = packed[...].T
    tq = jnp.concatenate([flipped[0:64, 0:256], flipped[64:128, 0:256]], axis=1)
    tk = jnp.concatenate([flipped[0:64, 256:384], flipped[64:128, 256:384]], axis=1)
    image_t[:, 0:RQ] = tq
    image_t[:, RQ:ROWS] = tk
    image_h[0:64, :] = image_t[...].astype(BF16)
    image_h[64:128, :] = (image_t[...] - image_h[0:64, :].astype(F32)).astype(BF16)

    high = lax.Precision.HIGHEST
    gsend[...] = jnp.concatenate([dot(tq, tq, 1, 1, high), dot(tk, tk, 1, 1, high)], axis=1)
    send(gsend, gsib, s_g, r_g, device(dc=1))

    def project(start):
        cols = at(start, PART, 128)
        q = dot(image_h[:, 0:RQ], merged[0:RQ, cols])
        k = dot(image_h[:, RQ:ROWS], merged[RQ:ROWS, cols])
        return q[0:64] + q[64:128], k[0:64] + k[64:128]

    for k in range(3):
        q, kk = project((1 - c) * HALF + PART * k)
        psend[k, 0:64, :] = q.astype(BF16)
        psend[k, 64:128, :] = kk.astype(BF16)
        send(psend.at[k], psib.at[k], s_p.at[k], r_p.at[k], device(dc=1))

    arrived(gsib, r_g, s_g)
    gx[x] = gsend[...] + gsib[...]
    for d in (1, 2, 3):
        send(gx.at[x], gx.at[x], s_gx, r_gx, device(dx=d))

    place = ((z, y, x), (z, x, y), (y, x, z))

    def move(k, da, db):
        return (device(da, db, 0), device(da, 0, db), device(0, da, db))[k]

    def slice_of(a, b):
        return at(16 * (2 * a + lax.div(b, 2)), 16, 16), LANES * lax.rem(b, 2)

    around = [(da, db) for da in range(4) for db in range(4) if (da, db) != (0, 0)]
    for k in range(3):
        q, kk = project(c * HALF + PART * k)
        arrived(psib.at[k], r_p.at[k], s_p.at[k])
        pown[k, 0:64, :] = (q + psib[k, 0:64, :].astype(F32)).astype(BF16)
        pown[k, 64:128, :] = (kk + psib[k, 64:128, :].astype(F32)).astype(BF16)
        a, b, _ = place[k]
        for da, db in around:
            rows, lanes = slice_of(lax.rem(a + da, 4), lax.rem(b + db, 4))
            send(pown.at[k, rows, at(lanes, LANES, 128)], rs.at[k, 4 * a + b], s_rs.at[k], r_rs.at[k], move(k, da, db))
        rows, lanes = slice_of(a, b)
        rs[k, 4 * a + b] = pown[k, rows, at(lanes, LANES, 128)]

    arrived(gx.at[0:3], r_gx, s_gx)
    factorize((gx[0] + gx[1]) + (gx[2] + gx[3]), inv)

    for k in range(3):
        arrived(rs.at[k, 0:15], r_rs.at[k], s_rs.at[k])
        total = rs[k, 0].astype(F32)
        for s in range(1, 16):
            total += rs[k, s].astype(F32)
        m = place[k][2]
        ar3[k, m] = total.astype(BF16)
        for d in (1, 2, 3):
            to = (device(dx=d), device(dy=d), device(dz=d))[k]
            send(ar3.at[k, m], ar3.at[k, m], s_a3.at[k], r_a3.at[k], to)

    both = inv[...]
    bq = dot(image_t[:, 0:RQ], both[:, 0:64], 0, 1, high)
    bk = dot(image_t[:, RQ:ROWS], both[:, 64:128], 0, 1, high)
    basis[0:RQ, :] = bq.astype(BF16)
    basis[RQ:ROWS, :] = bk.astype(BF16)

    for k in range(3):
        arrived(ar3.at[k, 0:3], r_a3.at[k], s_a3.at[k])
        total = ar3[k, 0].astype(F32)
        for s in (1, 2, 3):
            total += ar3[k, s].astype(F32)
        a, b, _ = place[k]
        rows, lanes = slice_of(a, b)
        spot = (rows, at(c * HALF + PART * k + lanes, LANES, 128))
        psum[spot] = total.astype(BF16)
        for da, db in around:
            send(psum.at[spot], psum.at[spot], s_ag.at[k], r_ag.at[k], move(k, da, db))

    for k in range(3):
        arrived(rs.at[k, 0:15], r_ag.at[k], s_ag.at[k])
        cols = at(c * HALF + PART * k, PART, 128)
        send(psum.at[:, cols], psum.at[:, cols], s_fw.at[k], r_fw.at[k], device(dc=1))

    sent(gsend, r_g, s_g)
    sent(gx.at[0:3], r_gx, s_gx)
    for h in (0, 1):
        sent(ar1.at[h, 0:3], r_ar1.at[h], s_ar1.at[h])
        sent(ar2.at[h, 0:3], r_ar2.at[h], s_ar2.at[h])
    for k in range(3):
        sent(psend.at[k], r_p.at[k], s_p.at[k])
        sent(rs.at[k, 0:15], r_rs.at[k], s_rs.at[k])
        sent(ar3.at[k, 0:3], r_a3.at[k], s_a3.at[k])
        sent(rs.at[k, 0:15], r_ag.at[k], s_ag.at[k])
    for k in range(3):
        arrived(psend.at[k], r_fw.at[k], s_fw.at[k])
        sent(psend.at[k], r_fw.at[k], s_fw.at[k])


def reduce(gq, gk, eq, ek, fq, fk):
    dma, vmem = pltpu.SemaphoreType.DMA, pltpu.VMEM
    return pl.pallas_call(
        reduce_kernel,
        name="reduce",
        out_shape=(
            vmem((ROWS, D), BF16),
            vmem((ROWS, RANK), BF16),
            vmem((2 * RANK, D), BF16),
            vmem((RANK, 128), F32),
        ),
        in_specs=[pl.BlockSpec(memory_space=pltpu.HBM)] * 6,
        out_specs=(pl.BlockSpec(memory_space=vmem),) * 4,
        scratch_shapes=[
            vmem((ROWS, D), BF16),
            vmem((2, RANK, D), BF16),
            vmem((ROWS, RANK), F32),
            vmem((2, 4, 192, 128), BF16),
            vmem((2, 4, 192, 128), BF16),
            vmem((384, 128), F32),
            vmem((RANK, ROWS), F32),
            vmem((2 * RANK, ROWS), BF16),
            vmem((RANK, 128), F32),
            vmem((RANK, 128), F32),
            vmem((4, RANK, 128), F32),
            vmem((3, 128, PART), BF16),
            vmem((3, 128, PART), BF16),
            vmem((3, 128, PART), BF16),
            vmem((3, 16, 16, LANES), BF16),
            vmem((3, 4, 16, LANES), BF16),
            dma((CHUNKS,)), dma,
            dma((2,)), dma((2,)), dma((2,)), dma((2,)),
            dma, dma, dma, dma,
            dma((3,)), dma((3,)), dma((3,)), dma((3,)), dma((3,)), dma((3,)),
            dma((3,)), dma((3,)), dma((3,)), dma((3,)),
        ],
        compiler_params=pltpu.CompilerParams(
            collective_id=0, has_side_effects=True, vmem_limit_bytes=53 << 20
        ),
    )(gq, gk, eq, ek, fq, fk)


def refresh_kernel(merged, basis, psum, inv, error_q, error_k, new_q, new_k):
    both = inv[...]
    cols = at(pl.program_id(0) * CHUNK, CHUNK, 128)
    for side, rows, new, error in ((0, slice(0, RQ), new_q, error_q), (1, slice(RQ, ROWS), new_k, error_k)):
        w = both[:, 64 * side:64 * side + 64]
        hi = w.astype(BF16)
        lo = (w - hi.astype(F32)).astype(BF16)
        p = psum[64 * side:64 * side + 64, cols]
        factor = (dot(hi, p) + dot(lo, p)).astype(BF16)
        new[0] = factor
        approx = dot(basis[rows, :] * 0.0625, factor)
        error[0, 0] = (merged[rows, cols].astype(F32) - approx).astype(BF16)


def refresh(merged, basis, psum, inv):
    return pl.pallas_call(
        refresh_kernel,
        name="refresh",
        grid=(CHUNKS,),
        out_shape=(
            jax.ShapeDtypeStruct((1, 1, RQ, D), BF16),
            jax.ShapeDtypeStruct((1, 1, RK, D), BF16),
            jax.ShapeDtypeStruct((1, RANK, D), BF16),
            jax.ShapeDtypeStruct((1, RANK, D), BF16),
        ),
        in_specs=[pl.BlockSpec(memory_space=pltpu.VMEM)] * 4,
        out_specs=(
            pl.BlockSpec((1, 1, RQ, CHUNK), lambda i: (0, 0, 0, i)),
            pl.BlockSpec((1, 1, RK, CHUNK), lambda i: (0, 0, 0, i)),
            pl.BlockSpec((1, RANK, CHUNK), lambda i: (0, 0, i)),
            pl.BlockSpec((1, RANK, CHUNK), lambda i: (0, 0, i)),
        ),
        compiler_params=pltpu.CompilerParams(vmem_limit_bytes=24 << 20),
    )(merged, basis, psum, inv)


def body(grad_query, grad_key, error_query, error_key, factor_query, factor_key):
    fq, fk = jnp.swapaxes(factor_query, 1, 2), jnp.swapaxes(factor_key, 1, 2)
    kept = reduce(grad_query, grad_key, error_query, error_key, fq, fk)
    new_eq, new_ek, new_q, new_k = refresh(*kept)
    return new_eq, new_ek, jnp.swapaxes(new_q, 1, 2), jnp.swapaxes(new_k, 1, 2)


def solution(mesh):
    split = P("dp", None, "tensor", None)
    return jax.shard_map(
        body,
        mesh=mesh,
        in_specs=(split, split, split, split, P(), P()),
        out_specs=(split, split, P(), P()),
        check_vma=False,
    )
```

time: 281 us -> 52.9 us (0.19)
  blocking collectives: 122 us -> 0 us
  waiting for transfers between devices: 85.8 us -> 0 us
  Pallas kernels: 0 us -> 52.2 us
  matrix products: 31.7 us -> 0 us
  other arithmetic: 24.2 us -> 0 us
  between operations: 14.1 us -> 0.64 us
    psum x2 -> x0, blocking collectives: 122 us -> none  [the longest x1 99.2 us: body(): lax.psum((projected(merged_q, basis_q), projected(merged_k, basis_k)), ('...]
    psum x1 -> x0, waiting for transfers between devices: 85.8 us -> none  [body(): image_q, image_k = lax.psum((image_q, image_k), 'dp')]
    pallas_call x0 -> x2, Pallas kernels: none -> 52.2 us  [the longest x1 46.3 us: reduce(): pl.pallas_call(reduce_kernel, name='reduce', out_shape=(vmem((ROWS, D), B...]
    dot_general x8 -> x0, matrix products: 30.3 us -> none  [the longest x2 10.7 us: refresh(): jnp.einsum('lhr,ldr->lhd', basis, factor, preferred_element_type=jnp.floa...]
    another operation x10 -> x0, other arithmetic: 24.1 us -> none  [the longest x6 13 us: orthonormal(): lower = jnp.linalg.cholesky(gram)]
  transfers between devices with their start and end apart: 1 -> 0, of which waited for: 1 -> 0; matrix products, arithmetic and copies ran while one was open for 0% -> 0% of each run, Pallas kernels for 0% -> 0%
where the time goes in v1:
time: 52.9 us; the launch traced here: 52.8 us
  Pallas kernels  52.2 us (99%)
  between operations  0.64 us (1%)
    pallas_call x1, Pallas kernels, reduce(): pl.pallas_call(reduce_kernel, name='reduce', out_shape=(vmem((ROWS, D), B...  46.3 us
    pallas_call x1, Pallas kernels, refresh(): pl.pallas_call(refresh_kernel, name='refresh', grid=(CHUNKS,), out_shape=...  5.83 us

profile of v1, /device:TPU:1, one launch (start us, length us, event | category | flops | bytes accessed | tf_op | source)
XLA Modules:
  0.0 52.8 jit_solution(10304860241058252787)
XLA Ops:
  0.6 46.3 %reduce.1 = (bf16[768,4608]{1,0:T(8,128)(2,1)S(1)}, bf16[768,64]{1,0:T(8,128)(2,1)S(1)}, bf16[128,4608]{1,0:T(8,128)(2,1)S(1)}, f32[64,128]{1,0:T(8,128)S(1)}) custom-call(bf16[1,1,512,4608]{3,2,1,0:T(8,128)(2,1)} %gq.1, bf16[1,1,256,4608]{3,2,1,0:T(8,128)(2,1)} %gk.1, bf16[1,1,512,4608]{3,2,1,0:T(8,128)(2,1)} %eq.1, bf16[1,1,256,4608]{3,2,1,0:T(8,128)(2,1)} %ek.1, ...), custom_call_target="tpu_custom_call" | custom-call | tf_op jit(solution)/shard_map/reduce/pallas_call | solution.py:248
  47.0 5.8 %refresh.1 = (bf16[1,1,512,4608]{3,2,1,0:T(8,128)(2,1)}, bf16[1,1,256,4608]{3,2,1,0:T(8,128)(2,1)}, bf16[1,64,4608]{2,1,0:T(8,128)(2,1)}, bf16[1,64,4608]{2,1,0:T(8,128)(2,1)}) custom-call(bf16[768,4608]{1,0:T(8,128)(2,1)S(1)} %get-tuple-element.12.merged, bf16[768,64]{1,0:T(8,128)(2,1)S(1)} %get-tuple-element.13.basis, ...), custom_call_target="tpu_custom_call" | custom-call | tf_op jit(solution)/shard_map/refresh/pallas_call | solution.py:303

commit v2 on v1

v2 whole, which is shorter than its diff:
```python
import jax
import jax.numpy as jnp
from jax import lax
from jax.experimental import pallas as pl
from jax.experimental.pallas import tpu as pltpu
from jax.sharding import PartitionSpec as P

F32, BF16 = jnp.float32, jnp.bfloat16
D, RANK = 4608, 64
RQ, RK = 512, 256
ROWS = RQ + RK
LOADS, WIDE = 3, D // 3
HALF = D // 2
PART = HALF // 3
LANES = PART // 2
MESH = pl.DeviceIdType.MESH


def dot(a, b, ca=1, cb=0, precision=None):
    return lax.dot_general(a, b, (((ca,), (cb,)), ((), ())), precision=precision, preferred_element_type=F32)


def at(start, size, unit):
    return pl.ds(pl.multiple_of(start, unit), size)


def factorize(gram, inv):
    lane = lax.broadcasted_iota(jnp.int32, (8, 128), 1)
    row = lax.broadcasted_iota(jnp.int32, (8, 128), 0)
    side = jnp.where(lane >= RANK, RANK, 0)
    for i in range(8):
        inv[8 * i:8 * i + 8, :] = jnp.where(lane - side == row + 8 * i, 1.0, 0.0).astype(F32)

    def column(x, j):
        return jnp.take_along_axis(x, side + j, axis=1, mode="promise_in_bounds")

    def block(b, carry):
        here = at(8 * b, 8, 8)
        g = [gram[here, :]] + [gram[8 * i:8 * i + 8, :] for i in range(8)]
        w = [inv[here, :]] + [inv[8 * i:8 * i + 8, :] for i in range(8)]
        done = [None] * 8
        for t in range(8):
            row_g = jnp.broadcast_to(g[0][t:t + 1, :], (8, 128))
            row_w = jnp.broadcast_to(w[0][t:t + 1, :], (8, 128))
            pivot = column(row_g, 8 * b + t)
            inverse = 1.0 / pivot
            done[t] = row_w * lax.rsqrt(pivot)
            scaled_g, scaled_w = row_g * inverse, row_w * inverse
            for i in range(9):
                below = row > t if i == 0 else i - 1 > b
                q = jnp.where(below, column(g[i], 8 * b + t), 0.0)
                g[i] = g[i] - q * scaled_g
                w[i] = w[i] - q * scaled_w
        last = done[0]
        for t in range(1, 8):
            last = jnp.where(row == t, done[t], last)
        for i in range(8):
            gram[8 * i:8 * i + 8, :] = g[i + 1]
            inv[8 * i:8 * i + 8, :] = w[i + 1]
        inv[here, :] = last
        return carry

    lax.fori_loop(0, 8, block, 0)


def subtract(source, target, basis, factor, start, into):
    cols, there = at(start, PART, 128), at(into, PART, 128)
    for side, rows in ((0, slice(0, RQ)), (1, slice(RQ, ROWS))):
        approx = dot(basis[rows, :], factor[64 * side:64 * side + 64, cols])
        target[rows, there] = (source[rows, cols].astype(F32) - approx).astype(BF16)


def reduce_kernel(gq, gk, eq, ek, fq, fk, merged, basis, factor,
                  psum, inv, white, ebuf, fbuf, acc, ar1, ar2, packed, image_t, image_h,
                  gsend, gsib, gx, psend, psib, pown, rs, ar3,
                  lsem, fsem, s_ar1, r_ar1, s_ar2, r_ar2, s_g, r_g, s_gx, r_gx,
                  s_p, r_p, s_rs, r_rs, s_a3, r_a3, s_ag, r_ag, s_fw, r_fw):
    dp, tensor = lax.axis_index("dp"), lax.axis_index("tensor")
    z, y = lax.div(dp, 4), lax.rem(dp, 4)
    x, c = lax.div(tensor, 2), lax.rem(tensor, 2)

    def device(dz=0, dy=0, dx=0, dc=0):
        return (lax.rem(z + dz, 4) * 4 + lax.rem(y + dy, 4), lax.rem(x + dx, 4) * 2 + lax.rem(c + dc, 2))

    def send(src, dst, ssem, rsem, to):
        pltpu.make_async_remote_copy(src, dst, ssem, rsem, device_id=to, device_id_type=MESH).start()

    def arrived(ref, rsem, ssem):
        pltpu.make_async_remote_copy(ref, ref, ssem, rsem, device_id=device(dc=1), device_id_type=MESH).wait_recv()

    def sent(ref, rsem, ssem):
        pltpu.make_async_remote_copy(ref, ref, ssem, rsem, device_id=device(dc=1), device_id_type=MESH).wait_send()

    loads = [
        pltpu.make_async_copy(fq.at[0], fbuf.at[0], fsem),
        pltpu.make_async_copy(fk.at[0], fbuf.at[1], fsem),
    ]
    for cp in loads:
        cp.start()

    def load(k):
        cols = at(k * WIDE, WIDE, 128)
        return [
            pltpu.make_async_copy(gq.at[0, 0, :, cols], merged.at[0:RQ, cols], lsem.at[k]),
            pltpu.make_async_copy(eq.at[0, 0, :, cols], ebuf.at[0:RQ, cols], lsem.at[k]),
            pltpu.make_async_copy(gk.at[0, 0, :, cols], merged.at[RQ:ROWS, cols], lsem.at[k]),
            pltpu.make_async_copy(ek.at[0, 0, :, cols], ebuf.at[RQ:ROWS, cols], lsem.at[k]),
        ]

    for k in range(LOADS):
        for cp in load(k):
            cp.start()

    offsets = [(a, b, d) for a in range(4) for b in range(4) for d in range(4) if (a, b, d) != (0, 0, 0) and 0 in (a, b, d)]
    barrier = pltpu.get_barrier_semaphore()
    peers = [device(a, b, d) for a, b, d in offsets] + [device(dc=1)]
    for to in peers:
        pl.semaphore_signal(barrier, 1, device_id=to, device_id_type=MESH)

    acc[...] = jnp.zeros_like(acc)
    for cp in loads:
        cp.wait()

    def merge(k, carry):
        cols = at(k * WIDE, WIDE, 128)
        for cp in load(k):
            cp.wait()
        merged[:, cols] = (merged[:, cols].astype(F32) + ebuf[:, cols].astype(F32)).astype(BF16)
        acc[0:RQ, :] += dot(merged[0:RQ, cols], fbuf[0, :, cols], 1, 1)
        acc[RQ:ROWS, :] += dot(merged[RQ:ROWS, cols], fbuf[1, :, cols], 1, 1)
        return carry

    lax.fori_loop(0, LOADS, merge, 0)

    halves = (ar1.at[0, z], ar1.at[1, y])
    top = jnp.concatenate([acc[0:256, :], acc[256:512, :]], axis=1).astype(BF16)
    low = jnp.concatenate([acc[512:640, :], acc[640:768, :]], axis=1).astype(BF16)
    halves[0][...] = top[0:192]
    halves[1][0:64, :] = top[192:256]
    halves[1][64:192, :] = low
    pl.semaphore_wait(barrier, len(peers))
    for d in (1, 2, 3):
        send(ar1.at[0, z], ar1.at[0, z], s_ar1.at[0], r_ar1.at[0], device(dz=d))
        send(ar1.at[1, y], ar1.at[1, y], s_ar1.at[1], r_ar1.at[1], device(dy=d))
    for h, mine in ((0, y), (1, z)):
        arrived(ar1.at[h, 0:3], r_ar1.at[h], s_ar1.at[h])
        total = ar1[h, 0].astype(F32)
        for s in (1, 2, 3):
            total += ar1[h, s].astype(F32)
        ar2[h, mine] = total.astype(BF16)
        for d in (1, 2, 3):
            to = device(dy=d) if h == 0 else device(dz=d)
            send(ar2.at[h, mine], ar2.at[h, mine], s_ar2.at[h], r_ar2.at[h], to)
    for h in (0, 1):
        arrived(ar2.at[h, 0:3], r_ar2.at[h], s_ar2.at[h])
        total = ar2[h, 0].astype(F32)
        for s in (1, 2, 3):
            total += ar2[h, s].astype(F32)
        packed[192 * h:192 * h + 192, :] = total

    flipped = packed[...].T
    tq = jnp.concatenate([flipped[0:64, 0:256], flipped[64:128, 0:256]], axis=1)
    tk = jnp.concatenate([flipped[0:64, 256:384], flipped[64:128, 256:384]], axis=1)
    image_t[:, 0:RQ] = tq
    image_t[:, RQ:ROWS] = tk
    image_h[0:64, :] = image_t[...].astype(BF16)
    image_h[64:128, :] = (image_t[...] - image_h[0:64, :].astype(F32)).astype(BF16)

    def project(start):
        cols = at(start, PART, 128)
        q = dot(image_h[:, 0:RQ], merged[0:RQ, cols])
        k = dot(image_h[:, RQ:ROWS], merged[RQ:ROWS, cols])
        return q[0:64] + q[64:128], k[0:64] + k[64:128]

    def split(k):
        first, last = lax.div(2 - k, 2), lax.div(k, 2)
        return first, 1 - first - last, last

    def place(k):
        first, middle, last = split(k)
        return z * (1 - last) + y * last, y * first + x * (1 - first), x * first + y * middle + z * last

    def move(k, da, db):
        first, middle, last = split(k)
        return device(da * (1 - last), db * first + da * last, db * (1 - first))

    def along(k, d):
        first, middle, last = split(k)
        return device(d * last, d * middle, d * first)

    def slice_of(a, b):
        return at(16 * (2 * a + lax.div(b, 2)), 16, 16), LANES * lax.rem(b, 2)

    around = [(da, db) for da in range(4) for db in range(4) if (da, db) != (0, 0)]

    def share(n, carry):
        @pl.when(n < 3)
        def _():
            q, kk = project((1 - c) * HALF + PART * n)
            psend[n, 0:64, :] = q.astype(BF16)
            psend[n, 64:128, :] = kk.astype(BF16)
            send(psend.at[n], psib.at[n], s_p.at[n], r_p.at[n], device(dc=1))

        @pl.when(n > 0)
        def _():
            k = n - 1
            q, kk = project(c * HALF + PART * k)
            arrived(psib.at[k], r_p.at[k], s_p.at[k])
            pown[k, 0:64, :] = (q + psib[k, 0:64, :].astype(F32)).astype(BF16)
            pown[k, 64:128, :] = (kk + psib[k, 64:128, :].astype(F32)).astype(BF16)
            a, b, _ = place(k)
            for da, db in around:
                rows, lanes = slice_of(lax.rem(a + da, 4), lax.rem(b + db, 4))
                send(pown.at[k, rows, at(lanes, LANES, 128)], rs.at[k, 4 * a + b], s_rs.at[k], r_rs.at[k], move(k, da, db))
            rows, lanes = slice_of(a, b)
            rs[k, 4 * a + b] = pown[k, rows, at(lanes, LANES, 128)]

        return carry

    lax.fori_loop(0, 4, share, 0)

    high = lax.Precision.HIGHEST
    tq, tk = image_t[:, 0:RQ], image_t[:, RQ:ROWS]
    gsend[...] = jnp.concatenate([dot(tq, tq, 1, 1, high), dot(tk, tk, 1, 1, high)], axis=1)
    send(gsend, gsib, s_g, r_g, device(dc=1))
    arrived(gsib, r_g, s_g)
    gx[x] = gsend[...] + gsib[...]
    for d in (1, 2, 3):
        send(gx.at[x], gx.at[x], s_gx, r_gx, device(dx=d))

    def gather(k, carry):
        arrived(rs.at[k, 0:15], r_rs.at[k], s_rs.at[k])
        total = rs[k, 0].astype(F32)
        for s in range(1, 16):
            total += rs[k, s].astype(F32)
        m = place(k)[2]
        ar3[k, m] = total.astype(BF16)
        for d in (1, 2, 3):
            send(ar3.at[k, m], ar3.at[k, m], s_a3.at[k], r_a3.at[k], along(k, d))
        return carry

    lax.fori_loop(0, 3, gather, 0)

    def spread(k, carry):
        arrived(ar3.at[k, 0:3], r_a3.at[k], s_a3.at[k])
        total = ar3[k, 0].astype(F32)
        for s in (1, 2, 3):
            total += ar3[k, s].astype(F32)
        a, b, _ = place(k)
        rows, lanes = slice_of(a, b)
        spot = (rows, at(c * HALF + PART * k + lanes, LANES, 128))
        psum[spot] = total.astype(BF16)
        for da, db in around:
            send(psum.at[spot], psum.at[spot], s_ag.at[k], r_ag.at[k], move(k, da, db))
        return carry

    lax.fori_loop(0, 3, spread, 0)

    arrived(gx.at[0:3], r_gx, s_gx)
    gsib[...] = (gx[0] + gx[1]) + (gx[2] + gx[3])
    factorize(gsib, inv)
    both = inv[...]
    for side, rows in ((0, slice(0, RQ)), (1, slice(RQ, ROWS))):
        w = both[:, 64 * side:64 * side + 64]
        basis[rows, :] = dot(image_t[:, rows], w, 0, 1, high).astype(BF16) * 0.0625
        hi = w.astype(BF16)
        white[side, 0:64] = hi
        white[side, 64:128] = (w - hi.astype(F32)).astype(BF16)

    def whiten(k, carry):
        arrived(rs.at[k, 0:15], r_ag.at[k], s_ag.at[k])
        cols = at(c * HALF + PART * k, PART, 128)
        for side in (0, 1):
            f = dot(white[side], psum[64 * side:64 * side + 64, cols])
            factor[64 * side:64 * side + 64, cols] = (f[0:64] + f[64:128]).astype(BF16)
        send(factor.at[:, cols], factor.at[:, cols], s_fw.at[k], r_fw.at[k], device(dc=1))
        return carry

    lax.fori_loop(0, 3, whiten, 0)

    def errors(k, carry):
        start = c * HALF + PART * k
        subtract(merged, merged, basis, factor, start, start)
        return carry

    lax.fori_loop(0, 3, errors, 0)

    sent(gsend, r_g, s_g)
    sent(gx.at[0:3], r_gx, s_gx)
    for h in (0, 1):
        sent(ar1.at[h, 0:3], r_ar1.at[h], s_ar1.at[h])
        sent(ar2.at[h, 0:3], r_ar2.at[h], s_ar2.at[h])
    for k in range(3):
        sent(psend.at[k], r_p.at[k], s_p.at[k])
        sent(rs.at[k, 0:15], r_rs.at[k], s_rs.at[k])
        sent(ar3.at[k, 0:3], r_a3.at[k], s_a3.at[k])
        sent(rs.at[k, 0:15], r_ag.at[k], s_ag.at[k])
    for k in range(3):
        arrived(psend.at[k], r_fw.at[k], s_fw.at[k])
        sent(psend.at[k], r_fw.at[k], s_fw.at[k])


def reduce(gq, gk, eq, ek, fq, fk):
    dma, vmem = pltpu.SemaphoreType.DMA, pltpu.VMEM
    return pl.pallas_call(
        reduce_kernel,
        name="reduce",
        out_shape=(
            vmem((ROWS, D), BF16),
            vmem((ROWS, RANK), BF16),
            vmem((2 * RANK, D), BF16),
        ),
        in_specs=[pl.BlockSpec(memory_space=pltpu.HBM)] * 6,
        out_specs=(pl.BlockSpec(memory_space=vmem),) * 3,
        scratch_shapes=[
            vmem((2 * RANK, D), BF16),
            vmem((RANK, 128), F32),
            vmem((2, 128, RANK), BF16),
            vmem((ROWS, D), BF16),
            vmem((2, RANK, D), BF16),
            vmem((ROWS, RANK), F32),
            vmem((2, 4, 192, 128), BF16),
            vmem((2, 4, 192, 128), BF16),
            vmem((384, 128), F32),
            vmem((RANK, ROWS), F32),
            vmem((2 * RANK, ROWS), BF16),
            vmem((RANK, 128), F32),
            vmem((RANK, 128), F32),
            vmem((4, RANK, 128), F32),
            vmem((3, 128, PART), BF16),
            vmem((3, 128, PART), BF16),
            vmem((3, 128, PART), BF16),
            vmem((3, 16, 16, LANES), BF16),
            vmem((3, 4, 16, LANES), BF16),
            dma((LOADS,)), dma,
            dma((2,)), dma((2,)), dma((2,)), dma((2,)),
            dma, dma, dma, dma,
            dma((3,)), dma((3,)), dma((3,)), dma((3,)), dma((3,)), dma((3,)),
            dma((3,)), dma((3,)), dma((3,)), dma((3,)),
        ],
        compiler_params=pltpu.CompilerParams(
            collective_id=0, has_side_effects=True, vmem_limit_bytes=53 << 20
        ),
    )(gq, gk, eq, ek, fq, fk)


def refresh_kernel(merged, basis, factor, error_q, error_k, new_q, new_k, buf, sem):
    c = lax.rem(lax.axis_index("tensor"), 2)
    own, other = c * HALF, (1 - c) * HALF
    mine = at(own, HALF, 128)
    copies = [
        pltpu.make_async_copy(merged.at[0:RQ, mine], error_q.at[0, 0, :, mine], sem.at[0]),
        pltpu.make_async_copy(merged.at[RQ:ROWS, mine], error_k.at[0, 0, :, mine], sem.at[1]),
        pltpu.make_async_copy(factor.at[0:RANK], new_q.at[0], sem.at[2]),
        pltpu.make_async_copy(factor.at[RANK:2 * RANK], new_k.at[0], sem.at[3]),
    ]
    for cp in copies:
        cp.start()
    def part(k):
        here, there = at(PART * k, PART, 128), at(other + PART * k, PART, 128)
        return [
            pltpu.make_async_copy(buf.at[0:RQ, here], error_q.at[0, 0, :, there], sem.at[4 + 2 * k]),
            pltpu.make_async_copy(buf.at[RQ:ROWS, here], error_k.at[0, 0, :, there], sem.at[5 + 2 * k]),
        ]

    def errors(k, carry):
        subtract(merged, buf, basis, factor, other + PART * k, PART * k)
        for cp in part(k):
            cp.start()
        return carry

    lax.fori_loop(0, 3, errors, 0)
    for k in range(3):
        copies += part(k)
    for cp in copies:
        cp.wait()


def refresh(merged, basis, factor):
    return pl.pallas_call(
        refresh_kernel,
        name="refresh",
        out_shape=(
            jax.ShapeDtypeStruct((1, 1, RQ, D), BF16),
            jax.ShapeDtypeStruct((1, 1, RK, D), BF16),
            jax.ShapeDtypeStruct((1, RANK, D), BF16),
            jax.ShapeDtypeStruct((1, RANK, D), BF16),
        ),
        in_specs=[pl.BlockSpec(memory_space=pltpu.VMEM)] * 3,
        out_specs=(pl.BlockSpec(memory_space=pltpu.HBM),) * 4,
        scratch_shapes=[pltpu.VMEM((ROWS, HALF), BF16), pltpu.SemaphoreType.DMA((10,))],
        compiler_params=pltpu.CompilerParams(vmem_limit_bytes=16 << 20),
    )(merged, basis, factor)


def body(grad_query, grad_key, error_query, error_key, factor_query, factor_key):
    fq, fk = jnp.swapaxes(factor_query, 1, 2), jnp.swapaxes(factor_key, 1, 2)
    kept = reduce(grad_query, grad_key, error_query, error_key, fq, fk)
    new_eq, new_ek, new_q, new_k = refresh(*kept)
    return new_eq, new_ek, jnp.swapaxes(new_q, 1, 2), jnp.swapaxes(new_k, 1, 2)


def solution(mesh):
    split = P("dp", None, "tensor", None)
    return jax.shard_map(
        body,
        mesh=mesh,
        in_specs=(split, split, split, split, P(), P()),
        out_specs=(split, split, P(), P()),
        check_vma=False,
    )
```

time: 52.9 us -> 49.3 us (0.932)
  Pallas kernels: 52.2 us -> 48.6 us
    pallas_call x1, Pallas kernels: 5.83 us -> 3.34 us  [refresh(): pl.pallas_call(refresh_kernel, name='refresh', out_shape=(jax.ShapeDtypeS...]
    pallas_call x1, Pallas kernels: 46.3 us -> 45.2 us  [reduce(): pl.pallas_call(reduce_kernel, name='reduce', out_shape=(vmem((ROWS, D), B...]
where the time goes in v2:
time: 49.3 us; the launch traced here: 49.2 us
  Pallas kernels  48.6 us (99%)
  between operations  0.64 us (1%)
    pallas_call x1, Pallas kernels, reduce(): pl.pallas_call(reduce_kernel, name='reduce', out_shape=(vmem((ROWS, D), B...  45.2 us
    pallas_call x1, Pallas kernels, refresh(): pl.pallas_call(refresh_kernel, name='refresh', out_shape=(jax.ShapeDtypeS...  3.34 us

profile of v2, /device:TPU:1, one launch (start us, length us, event | category | flops | bytes accessed | tf_op | source)
XLA Modules:
  0.0 49.2 jit_solution(6408187503669859829)
XLA Ops:
  0.6 45.2 %reduce.1 = (bf16[768,4608]{1,0:T(8,128)(2,1)S(1)}, bf16[768,64]{1,0:T(8,128)(2,1)S(1)}, bf16[128,4608]{1,0:T(8,128)(2,1)S(1)}) custom-call(bf16[1,1,512,4608]{3,2,1,0:T(8,128)(2,1)} %gq.1, bf16[1,1,256,4608]{3,2,1,0:T(8,128)(2,1)} %gk.1, bf16[1,1,512,4608]{3,2,1,0:T(8,128)(2,1)} %eq.1, bf16[1,1,256,4608]{3,2,1,0:T(8,128)(2,1)} %ek.1, ...), custom_call_target="tpu_custom_call" | custom-call | tf_op jit(solution)/shard_map/reduce/pallas_call | solution.py:305
  45.9 3.3 %refresh.1 = (bf16[1,1,512,4608]{3,2,1,0:T(8,128)(2,1)}, bf16[1,1,256,4608]{3,2,1,0:T(8,128)(2,1)}, bf16[1,64,4608]{2,1,0:T(8,128)(2,1)}, bf16[1,64,4608]{2,1,0:T(8,128)(2,1)}) custom-call(bf16[768,4608]{1,0:T(8,128)(2,1)S(1)} %get-tuple-element.11.merged, bf16[768,64]{1,0:T(8,128)(2,1)S(1)} %get-tuple-element.12.basis, ...), custom_call_target="tpu_custom_call" | custom-call | tf_op jit(solution)/shard_map/refresh/pallas_call | solution.py:380

commit v3 on v2

--- a/solution.py
+++ b/solution.py
@@ -39,18 +39,26 @@
         g = [gram[here, :]] + [gram[8 * i:8 * i + 8, :] for i in range(8)]
         w = [inv[here, :]] + [inv[8 * i:8 * i + 8, :] for i in range(8)]
         done = [None] * 8
-        for t in range(8):
-            row_g = jnp.broadcast_to(g[0][t:t + 1, :], (8, 128))
-            row_w = jnp.broadcast_to(w[0][t:t + 1, :], (8, 128))
-            pivot = column(row_g, 8 * b + t)
-            inverse = 1.0 / pivot
-            done[t] = row_w * lax.rsqrt(pivot)
-            scaled_g, scaled_w = row_g * inverse, row_w * inverse
+        for t in range(0, 8, 2):
+            j = 8 * b + t
+            row_g0, row_g1 = (jnp.broadcast_to(g[0][r:r + 1, :], (8, 128)) for r in (t, t + 1))
+            row_w0, row_w1 = (jnp.broadcast_to(w[0][r:r + 1, :], (8, 128)) for r in (t, t + 1))
+            pivot0, beside, pivot1 = column(row_g0, j), column(row_g0, j + 1), column(row_g1, j + 1)
+            inverse0 = 1.0 / pivot0
+            ratio = beside * inverse0
+            pivot1 = pivot1 - ratio * beside
+            inverse1 = 1.0 / pivot1
+            row_g1, row_w1 = row_g1 - ratio * row_g0, row_w1 - ratio * row_w0
+            done[t], done[t + 1] = row_w0 * lax.rsqrt(pivot0), row_w1 * lax.rsqrt(pivot1)
+            scaled_g0, scaled_w0 = row_g0 * inverse0, row_w0 * inverse0
+            scaled_g1, scaled_w1 = row_g1 * inverse1, row_w1 * inverse1
             for i in range(9):
-                below = row > t if i == 0 else i - 1 > b
-                q = jnp.where(below, column(g[i], 8 * b + t), 0.0)
-                g[i] = g[i] - q * scaled_g
-                w[i] = w[i] - q * scaled_w
+                c0, c1 = column(g[i], j), column(g[i], j + 1)
+                c1 = c1 - ratio * c0
+                c0 = jnp.where(row > t if i == 0 else i - 1 > b, c0, 0.0)
+                c1 = jnp.where(row > t + 1 if i == 0 else i - 1 > b, c1, 0.0)
+                g[i] = g[i] - c0 * scaled_g0 - c1 * scaled_g1
+                w[i] = w[i] - c0 * scaled_w0 - c1 * scaled_w1
         last = done[0]
         for t in range(1, 8):
             last = jnp.where(row == t, done[t], last)
@@ -71,7 +79,7 @@
 
 
 def reduce_kernel(gq, gk, eq, ek, fq, fk, merged, basis, factor,
-                  psum, inv, white, ebuf, fbuf, acc, ar1, ar2, packed, image_t, image_h,
+                  psum, inv, white, ebuf, fbuf, ar1, ar2, image_t, image_h,
                   gsend, gsib, gx, psend, psib, pown, rs, ar3,
                   lsem, fsem, s_ar1, r_ar1, s_ar2, r_ar2, s_g, r_g, s_gx, r_gx,
                   s_p, r_p, s_rs, r_rs, s_a3, r_a3, s_ag, r_ag, s_fw, r_fw):
@@ -117,7 +125,7 @@
     for to in peers:
         pl.semaphore_signal(barrier, 1, device_id=to, device_id_type=MESH)
 
-    acc[...] = jnp.zeros_like(acc)
+    image_t[...] = jnp.zeros_like(image_t)
     for cp in loads:
         cp.wait()
 
@@ -126,48 +134,45 @@
         for cp in load(k):
             cp.wait()
         merged[:, cols] = (merged[:, cols].astype(F32) + ebuf[:, cols].astype(F32)).astype(BF16)
-        acc[0:RQ, :] += dot(merged[0:RQ, cols], fbuf[0, :, cols], 1, 1)
-        acc[RQ:ROWS, :] += dot(merged[RQ:ROWS, cols], fbuf[1, :, cols], 1, 1)
+        image_t[:, 0:RQ] += dot(fbuf[0, :, cols], merged[0:RQ, cols], 1, 1)
+        image_t[:, RQ:ROWS] += dot(fbuf[1, :, cols], merged[RQ:ROWS, cols], 1, 1)
         return carry
 
     lax.fori_loop(0, LOADS, merge, 0)
 
-    halves = (ar1.at[0, z], ar1.at[1, y])
-    top = jnp.concatenate([acc[0:256, :], acc[256:512, :]], axis=1).astype(BF16)
-    low = jnp.concatenate([acc[512:640, :], acc[640:768, :]], axis=1).astype(BF16)
-    halves[0][...] = top[0:192]
-    halves[1][0:64, :] = top[192:256]
-    halves[1][64:192, :] = low
     pl.semaphore_wait(barrier, len(peers))
-    for d in (1, 2, 3):
-        send(ar1.at[0, z], ar1.at[0, z], s_ar1.at[0], r_ar1.at[0], device(dz=d))
-        send(ar1.at[1, y], ar1.at[1, y], s_ar1.at[1], r_ar1.at[1], device(dy=d))
-    for h, mine in ((0, y), (1, z)):
-        arrived(ar1.at[h, 0:3], r_ar1.at[h], s_ar1.at[h])
-        total = ar1[h, 0].astype(F32)
+    pieces = [(p, p % 2) for p in range(4)]
+    first, second = (z, y), (y, z)
+
+    def to(h, d):
+        return device(dz=d) if h == 0 else device(dy=d)
+
+    for p, h in pieces:
+        mine = ar1.at[p, first[h]]
+        mine[...] = image_t[16 * p:16 * p + 16, :].astype(BF16)
+        for d in (2, 1, 3):
+            send(mine, mine, s_ar1.at[p], r_ar1.at[p], to(h, d))
+    for p, h in pieces:
+        arrived(ar1.at[p, 0:3], r_ar1.at[p], s_ar1.at[p])
+        total = ar1[p, 0].astype(F32)
         for s in (1, 2, 3):
-            total += ar1[h, s].astype(F32)
-        ar2[h, mine] = total.astype(BF16)
-        for d in (1, 2, 3):
-            to = device(dy=d) if h == 0 else device(dz=d)
-            send(ar2.at[h, mine], ar2.at[h, mine], s_ar2.at[h], r_ar2.at[h], to)
-    for h in (0, 1):
-        arrived(ar2.at[h, 0:3], r_ar2.at[h], s_ar2.at[h])
-        total = ar2[h, 0].astype(F32)
+            total += ar1[p, s].astype(F32)
+        mine = ar2.at[p, second[h]]
+        mine[...] = total.astype(BF16)
+        for d in (2, 1, 3):
+            send(mine, mine, s_ar2.at[p], r_ar2.at[p], to(1 - h, d))
+    for p, h in pieces:
+        arrived(ar2.at[p, 0:3], r_ar2.at[p], s_ar2.at[p])
+        total = ar2[p, 0].astype(F32)
         for s in (1, 2, 3):
-            total += ar2[h, s].astype(F32)
-        packed[192 * h:192 * h + 192, :] = total
-
-    flipped = packed[...].T
-    tq = jnp.concatenate([flipped[0:64, 0:256], flipped[64:128, 0:256]], axis=1)
-    tk = jnp.concatenate([flipped[0:64, 256:384], flipped[64:128, 256:384]], axis=1)
-    image_t[:, 0:RQ] = tq
-    image_t[:, RQ:ROWS] = tk
+            total += ar2[p, s].astype(F32)
+        image_t[16 * p:16 * p + 16, :] = total
+
     image_h[0:64, :] = image_t[...].astype(BF16)
     image_h[64:128, :] = (image_t[...] - image_h[0:64, :].astype(F32)).astype(BF16)
 
-    def project(start):
-        cols = at(start, PART, 128)
+    def project(start, width=PART):
+        cols = at(start, width, 128)
         q = dot(image_h[:, 0:RQ], merged[0:RQ, cols])
         k = dot(image_h[:, RQ:ROWS], merged[RQ:ROWS, cols])
         return q[0:64] + q[64:128], k[0:64] + k[64:128]
@@ -192,32 +197,29 @@
         return at(16 * (2 * a + lax.div(b, 2)), 16, 16), LANES * lax.rem(b, 2)
 
     around = [(da, db) for da in range(4) for db in range(4) if (da, db) != (0, 0)]
-
-    def share(n, carry):
-        @pl.when(n < 3)
-        def _():
-            q, kk = project((1 - c) * HALF + PART * n)
-            psend[n, 0:64, :] = q.astype(BF16)
-            psend[n, 64:128, :] = kk.astype(BF16)
-            send(psend.at[n], psib.at[n], s_p.at[n], r_p.at[n], device(dc=1))
-
-        @pl.when(n > 0)
-        def _():
-            k = n - 1
-            q, kk = project(c * HALF + PART * k)
-            arrived(psib.at[k], r_p.at[k], s_p.at[k])
-            pown[k, 0:64, :] = (q + psib[k, 0:64, :].astype(F32)).astype(BF16)
-            pown[k, 64:128, :] = (kk + psib[k, 64:128, :].astype(F32)).astype(BF16)
-            a, b, _ = place(k)
-            for da, db in around:
-                rows, lanes = slice_of(lax.rem(a + da, 4), lax.rem(b + db, 4))
-                send(pown.at[k, rows, at(lanes, LANES, 128)], rs.at[k, 4 * a + b], s_rs.at[k], r_rs.at[k], move(k, da, db))
-            rows, lanes = slice_of(a, b)
-            rs[k, 4 * a + b] = pown[k, rows, at(lanes, LANES, 128)]
-
-        return carry
-
-    lax.fori_loop(0, 4, share, 0)
+    around.sort(key=lambda o: -(min(o[0], 4 - o[0]) + min(o[1], 4 - o[1])))
+
+    q, kk = project((1 - c) * HALF, HALF)
+    for n in range(3):
+        psend[n, 0:64, :] = q[:, PART * n:PART * n + PART].astype(BF16)
+        psend[n, 64:128, :] = kk[:, PART * n:PART * n + PART].astype(BF16)
+        send(psend.at[n], psib.at[n], s_p.at[n], r_p.at[n], device(dc=1))
+
+    def share(k, carry):
+        q, kk = project(c * HALF + PART * k)
+        arrived(psib.at[k], r_p.at[k], s_p.at[k])
+        pown[k, 0:64, :] = (q + psib[k, 0:64, :].astype(F32)).astype(BF16)
+        pown[k, 64:128, :] = (kk + psib[k, 64:128, :].astype(F32)).astype(BF16)
+        a, b, _ = place(k)
+        for da, db in around:
+            rows, lanes = slice_of(lax.rem(a + da, 4), lax.rem(b + db, 4))
+            send(pown.at[k, rows, at(lanes, LANES, 128)], rs.at[k, 4 * a + b], s_rs.at[k], r_rs.at[k], move(k, da, db))
+        rows, lanes = slice_of(a, b)
+        rs[k, 4 * a + b] = pown[k, rows, at(lanes, LANES, 128)]
+
+        return carry
+
+    lax.fori_loop(0, 3, share, 0)
 
     high = lax.Precision.HIGHEST
     tq, tk = image_t[:, 0:RQ], image_t[:, RQ:ROWS]
@@ -225,7 +227,7 @@
     send(gsend, gsib, s_g, r_g, device(dc=1))
     arrived(gsib, r_g, s_g)
     gx[x] = gsend[...] + gsib[...]
-    for d in (1, 2, 3):
+    for d in (2, 1, 3):
         send(gx.at[x], gx.at[x], s_gx, r_gx, device(dx=d))
 
     def gather(k, carry):
@@ -235,7 +237,7 @@
             total += rs[k, s].astype(F32)
         m = place(k)[2]
         ar3[k, m] = total.astype(BF16)
-        for d in (1, 2, 3):
+        for d in (2, 1, 3):
             send(ar3.at[k, m], ar3.at[k, m], s_a3.at[k], r_a3.at[k], along(k, d))
         return carry
 
@@ -287,9 +289,9 @@
 
     sent(gsend, r_g, s_g)
     sent(gx.at[0:3], r_gx, s_gx)
-    for h in (0, 1):
-        sent(ar1.at[h, 0:3], r_ar1.at[h], s_ar1.at[h])
-        sent(ar2.at[h, 0:3], r_ar2.at[h], s_ar2.at[h])
+    for p in range(4):
+        sent(ar1.at[p, 0:3], r_ar1.at[p], s_ar1.at[p])
+        sent(ar2.at[p, 0:3], r_ar2.at[p], s_ar2.at[p])
     for k in range(3):
         sent(psend.at[k], r_p.at[k], s_p.at[k])
         sent(rs.at[k, 0:15], r_rs.at[k], s_rs.at[k])
@@ -318,10 +320,8 @@
             vmem((2, 128, RANK), BF16),
             vmem((ROWS, D), BF16),
             vmem((2, RANK, D), BF16),
-            vmem((ROWS, RANK), F32),
-            vmem((2, 4, 192, 128), BF16),
-            vmem((2, 4, 192, 128), BF16),
-            vmem((384, 128), F32),
+            vmem((4, 4, 16, ROWS), BF16),
+            vmem((4, 4, 16, ROWS), BF16),
             vmem((RANK, ROWS), F32),
             vmem((2 * RANK, ROWS), BF16),
             vmem((RANK, 128), F32),
@@ -333,7 +333,7 @@
             vmem((3, 16, 16, LANES), BF16),
             vmem((3, 4, 16, LANES), BF16),
             dma((LOADS,)), dma,
-            dma((2,)), dma((2,)), dma((2,)), dma((2,)),
+            dma((4,)), dma((4,)), dma((4,)), dma((4,)),
             dma, dma, dma, dma,
             dma((3,)), dma((3,)), dma((3,)), dma((3,)), dma((3,)), dma((3,)),
             dma((3,)), dma((3,)), dma((3,)), dma((3,)),

time: 49.3 us -> 46.6 us (0.945)
  Pallas kernels: 48.6 us -> 45.8 us
    pallas_call x1, Pallas kernels: 45.2 us -> 42.5 us  [reduce(): pl.pallas_call(reduce_kernel, name='reduce', out_shape=(vmem((ROWS, D), B...]
where the time goes in v3:
time: 46.6 us; the launch traced here: 46.5 us
  Pallas kernels  45.8 us (98%)
  between operations  0.64 us (1%)
    pallas_call x1, Pallas kernels, reduce(): pl.pallas_call(reduce_kernel, name='reduce', out_shape=(vmem((ROWS, D), B...  42.5 us
    pallas_call x1, Pallas kernels, refresh(): pl.pallas_call(refresh_kernel, name='refresh', out_shape=(jax.ShapeDtypeS...  3.34 us

profile of v3, /device:TPU:1, one launch (start us, length us, event | category | flops | bytes accessed | tf_op | source)
XLA Modules:
  0.0 46.5 jit_solution(5541524995091585442)
XLA Ops:
  0.6 42.5 %reduce.1 = (bf16[768,4608]{1,0:T(8,128)(2,1)S(1)}, bf16[768,64]{1,0:T(8,128)(2,1)S(1)}, bf16[128,4608]{1,0:T(8,128)(2,1)S(1)}) custom-call(bf16[1,1,512,4608]{3,2,1,0:T(8,128)(2,1)} %gq.1, bf16[1,1,256,4608]{3,2,1,0:T(8,128)(2,1)} %gk.1, bf16[1,1,512,4608]{3,2,1,0:T(8,128)(2,1)} %eq.1, bf16[1,1,256,4608]{3,2,1,0:T(8,128)(2,1)} %ek.1, ...), custom_call_target="tpu_custom_call" | custom-call | tf_op jit(solution)/shard_map/reduce/pallas_call | solution.py:307
  43.1 3.3 %refresh.1 = (bf16[1,1,512,4608]{3,2,1,0:T(8,128)(2,1)}, bf16[1,1,256,4608]{3,2,1,0:T(8,128)(2,1)}, bf16[1,64,4608]{2,1,0:T(8,128)(2,1)}, bf16[1,64,4608]{2,1,0:T(8,128)(2,1)}) custom-call(bf16[768,4608]{1,0:T(8,128)(2,1)S(1)} %get-tuple-element.11.merged, bf16[768,64]{1,0:T(8,128)(2,1)S(1)} %get-tuple-element.12.basis, ...), custom_call_target="tpu_custom_call" | custom-call | tf_op jit(solution)/shard_map/refresh/pallas_call | solution.py:380

commit v4 on v3

--- a/solution.py
+++ b/solution.py
@@ -9,7 +9,8 @@
 D, RANK = 4608, 64
 RQ, RK = 512, 256
 ROWS = RQ + RK
-LOADS, WIDE = 3, D // 3
+BLOCK = 256
+BLOCKS = ROWS // BLOCK
 HALF = D // 2
 PART = HALF // 3
 LANES = PART // 2
@@ -106,18 +107,10 @@
     for cp in loads:
         cp.start()
 
-    def load(k):
-        cols = at(k * WIDE, WIDE, 128)
-        return [
-            pltpu.make_async_copy(gq.at[0, 0, :, cols], merged.at[0:RQ, cols], lsem.at[k]),
-            pltpu.make_async_copy(eq.at[0, 0, :, cols], ebuf.at[0:RQ, cols], lsem.at[k]),
-            pltpu.make_async_copy(gk.at[0, 0, :, cols], merged.at[RQ:ROWS, cols], lsem.at[k]),
-            pltpu.make_async_copy(ek.at[0, 0, :, cols], ebuf.at[RQ:ROWS, cols], lsem.at[k]),
-        ]
-
-    for k in range(LOADS):
-        for cp in load(k):
-            cp.start()
+    for k, (grad, error, row) in enumerate(((gq, eq, 0), (gq, eq, BLOCK), (gk, ek, 0))):
+        rows, there = pl.ds(row, BLOCK), pl.ds(BLOCK * k, BLOCK)
+        pltpu.make_async_copy(grad.at[0, 0, rows], merged.at[there], lsem.at[k]).start()
+        pltpu.make_async_copy(error.at[0, 0, rows], ebuf.at[there], lsem.at[k]).start()
 
     offsets = [(a, b, d) for a in range(4) for b in range(4) for d in range(4) if (a, b, d) != (0, 0, 0) and 0 in (a, b, d)]
     barrier = pltpu.get_barrier_semaphore()
@@ -125,48 +118,58 @@
     for to in peers:
         pl.semaphore_signal(barrier, 1, device_id=to, device_id_type=MESH)
 
-    image_t[...] = jnp.zeros_like(image_t)
+    first, second = (z, y), (y, z)
+
+    def to(h, d):
+        return device(dz=d) if h == 0 else device(dy=d)
+
     for cp in loads:
         cp.wait()
 
     def merge(k, carry):
-        cols = at(k * WIDE, WIDE, 128)
-        for cp in load(k):
-            cp.wait()
-        merged[:, cols] = (merged[:, cols].astype(F32) + ebuf[:, cols].astype(F32)).astype(BF16)
-        image_t[:, 0:RQ] += dot(fbuf[0, :, cols], merged[0:RQ, cols], 1, 1)
-        image_t[:, RQ:ROWS] += dot(fbuf[1, :, cols], merged[RQ:ROWS, cols], 1, 1)
-        return carry
-
-    lax.fori_loop(0, LOADS, merge, 0)
-
-    pl.semaphore_wait(barrier, len(peers))
-    pieces = [(p, p % 2) for p in range(4)]
-    first, second = (z, y), (y, z)
-
-    def to(h, d):
-        return device(dz=d) if h == 0 else device(dy=d)
-
-    for p, h in pieces:
-        mine = ar1.at[p, first[h]]
-        mine[...] = image_t[16 * p:16 * p + 16, :].astype(BF16)
-        for d in (2, 1, 3):
-            send(mine, mine, s_ar1.at[p], r_ar1.at[p], to(h, d))
-    for p, h in pieces:
-        arrived(ar1.at[p, 0:3], r_ar1.at[p], s_ar1.at[p])
-        total = ar1[p, 0].astype(F32)
-        for s in (1, 2, 3):
-            total += ar1[p, s].astype(F32)
-        mine = ar2.at[p, second[h]]
-        mine[...] = total.astype(BF16)
-        for d in (2, 1, 3):
-            send(mine, mine, s_ar2.at[p], r_ar2.at[p], to(1 - h, d))
-    for p, h in pieces:
-        arrived(ar2.at[p, 0:3], r_ar2.at[p], s_ar2.at[p])
-        total = ar2[p, 0].astype(F32)
-        for s in (1, 2, 3):
-            total += ar2[p, s].astype(F32)
-        image_t[16 * p:16 * p + 16, :] = total
+        rows = at(BLOCK * k, BLOCK, BLOCK)
+        pltpu.make_async_copy(gk.at[0, 0], merged.at[rows], lsem.at[k]).wait()
+        pltpu.make_async_copy(ek.at[0, 0], ebuf.at[rows], lsem.at[k]).wait()
+        merged[rows, :] = (merged[rows, :].astype(F32) + ebuf[rows, :].astype(F32)).astype(BF16)
+        part = dot(fbuf[lax.div(k, 2)], merged[rows, :], 1, 1)
+
+        @pl.when(k == 0)
+        def _():
+            pl.semaphore_wait(barrier, len(peers))
+
+        for h in (0, 1):
+            mine = ar1.at[k, h, first[h]]
+            mine[...] = part[32 * h:32 * h + 32].astype(BF16)
+            for d in (2, 1, 3):
+                send(mine, mine, s_ar1.at[k, h], r_ar1.at[k, h], to(h, d))
+        return carry
+
+    lax.fori_loop(0, BLOCKS, merge, 0)
+
+    def relay(k, carry):
+        for h in (0, 1):
+            arrived(ar1.at[k, h, 0:3], r_ar1.at[k, h], s_ar1.at[k, h])
+            total = ar1[k, h, 0].astype(F32)
+            for s in (1, 2, 3):
+                total += ar1[k, h, s].astype(F32)
+            mine = ar2.at[k, h, second[h]]
+            mine[...] = total.astype(BF16)
+            for d in (2, 1, 3):
+                send(mine, mine, s_ar2.at[k, h], r_ar2.at[k, h], to(1 - h, d))
+        return carry
+
+    lax.fori_loop(0, BLOCKS, relay, 0)
+
+    def finish(k, carry):
+        for h in (0, 1):
+            arrived(ar2.at[k, h, 0:3], r_ar2.at[k, h], s_ar2.at[k, h])
+            total = ar2[k, h, 0].astype(F32)
+            for s in (1, 2, 3):
+                total += ar2[k, h, s].astype(F32)
+            image_t[32 * h:32 * h + 32, at(BLOCK * k, BLOCK, BLOCK)] = total
+        return carry
+
+    lax.fori_loop(0, BLOCKS, finish, 0)
 
     image_h[0:64, :] = image_t[...].astype(BF16)
     image_h[64:128, :] = (image_t[...] - image_h[0:64, :].astype(F32)).astype(BF16)
@@ -289,9 +292,10 @@
 
     sent(gsend, r_g, s_g)
     sent(gx.at[0:3], r_gx, s_gx)
-    for p in range(4):
-        sent(ar1.at[p, 0:3], r_ar1.at[p], s_ar1.at[p])
-        sent(ar2.at[p, 0:3], r_ar2.at[p], s_ar2.at[p])
+    for k in range(BLOCKS):
+        for h in (0, 1):
+            sent(ar1.at[k, h, 0:3], r_ar1.at[k, h], s_ar1.at[k, h])
+            sent(ar2.at[k, h, 0:3], r_ar2.at[k, h], s_ar2.at[k, h])
     for k in range(3):
         sent(psend.at[k], r_p.at[k], s_p.at[k])
         sent(rs.at[k, 0:15], r_rs.at[k], s_rs.at[k])
@@ -320,8 +324,8 @@
             vmem((2, 128, RANK), BF16),
             vmem((ROWS, D), BF16),
             vmem((2, RANK, D), BF16),
-            vmem((4, 4, 16, ROWS), BF16),
-            vmem((4, 4, 16, ROWS), BF16),
+            vmem((BLOCKS, 2, 4, 32, BLOCK), BF16),
+            vmem((BLOCKS, 2, 4, 32, BLOCK), BF16),
             vmem((RANK, ROWS), F32),
             vmem((2 * RANK, ROWS), BF16),
             vmem((RANK, 128), F32),
@@ -332,8 +336,8 @@
             vmem((3, 128, PART), BF16),
             vmem((3, 16, 16, LANES), BF16),
             vmem((3, 4, 16, LANES), BF16),
-            dma((LOADS,)), dma,
-            dma((4,)), dma((4,)), dma((4,)), dma((4,)),
+            dma((BLOCKS,)), dma,
+            dma((BLOCKS, 2)), dma((BLOCKS, 2)), dma((BLOCKS, 2)), dma((BLOCKS, 2)),
             dma, dma, dma, dma,
             dma((3,)), dma((3,)), dma((3,)), dma((3,)), dma((3,)), dma((3,)),
             dma((3,)), dma((3,)), dma((3,)), dma((3,)),

time: 46.6 us -> 45.3 us (0.972)
  Pallas kernels: 45.8 us -> 44.6 us
    pallas_call x1, Pallas kernels: 42.5 us -> 41.2 us  [reduce(): pl.pallas_call(reduce_kernel, name='reduce', out_shape=(vmem((ROWS, D), B...]
where the time goes in v4:
time: 45.3 us; the launch traced here: 45.2 us
  Pallas kernels  44.6 us (98%)
  between operations  0.64 us (1%)
    pallas_call x1, Pallas kernels, reduce(): pl.pallas_call(reduce_kernel, name='reduce', out_shape=(vmem((ROWS, D), B...  41.2 us
    pallas_call x1, Pallas kernels, refresh(): pl.pallas_call(refresh_kernel, name='refresh', out_shape=(jax.ShapeDtypeS...  3.34 us

profile of v4, /device:TPU:1, one launch (start us, length us, event | category | flops | bytes accessed | tf_op | source)
XLA Modules:
  0.0 45.2 jit_solution(7132876964710660670)
XLA Ops:
  0.6 41.2 %reduce.1 = (bf16[768,4608]{1,0:T(8,128)(2,1)S(1)}, bf16[768,64]{1,0:T(8,128)(2,1)S(1)}, bf16[128,4608]{1,0:T(8,128)(2,1)S(1)}) custom-call(bf16[1,1,512,4608]{3,2,1,0:T(8,128)(2,1)} %gq.1, bf16[1,1,256,4608]{3,2,1,0:T(8,128)(2,1)} %gk.1, bf16[1,1,512,4608]{3,2,1,0:T(8,128)(2,1)} %eq.1, bf16[1,1,256,4608]{3,2,1,0:T(8,128)(2,1)} %ek.1, ...), custom_call_target="tpu_custom_call" | custom-call | tf_op jit(solution)/shard_map/reduce/pallas_call | solution.py:311
  41.9 3.3 %refresh.1 = (bf16[1,1,512,4608]{3,2,1,0:T(8,128)(2,1)}, bf16[1,1,256,4608]{3,2,1,0:T(8,128)(2,1)}, bf16[1,64,4608]{2,1,0:T(8,128)(2,1)}, bf16[1,64,4608]{2,1,0:T(8,128)(2,1)}) custom-call(bf16[768,4608]{1,0:T(8,128)(2,1)S(1)} %get-tuple-element.11.merged, bf16[768,64]{1,0:T(8,128)(2,1)S(1)} %get-tuple-element.12.basis, ...), custom_call_target="tpu_custom_call" | custom-call | tf_op jit(solution)/shard_map/refresh/pallas_call | solution.py:384

commit v5 on v4

--- a/solution.py
+++ b/solution.py
@@ -81,7 +81,7 @@
 
 def reduce_kernel(gq, gk, eq, ek, fq, fk, merged, basis, factor,
                   psum, inv, white, ebuf, fbuf, ar1, ar2, image_t, image_h,
-                  gsend, gsib, gx, psend, psib, pown, rs, ar3,
+                  gsend, gsib, gx, qown, psend, psib, pown, rs, ar3,
                   lsem, fsem, s_ar1, r_ar1, s_ar2, r_ar2, s_g, r_g, s_gx, r_gx,
                   s_p, r_p, s_rs, r_rs, s_a3, r_a3, s_ag, r_ag, s_fw, r_fw):
     dp, tensor = lax.axis_index("dp"), lax.axis_index("tensor")
@@ -169,16 +169,30 @@
             image_t[32 * h:32 * h + 32, at(BLOCK * k, BLOCK, BLOCK)] = total
         return carry
 
-    lax.fori_loop(0, BLOCKS, finish, 0)
-
-    image_h[0:64, :] = image_t[...].astype(BF16)
-    image_h[64:128, :] = (image_t[...] - image_h[0:64, :].astype(F32)).astype(BF16)
-
-    def project(start, width=PART):
-        cols = at(start, width, 128)
-        q = dot(image_h[:, 0:RQ], merged[0:RQ, cols])
-        k = dot(image_h[:, RQ:ROWS], merged[RQ:ROWS, cols])
-        return q[0:64] + q[64:128], k[0:64] + k[64:128]
+    query, key = slice(0, RQ), slice(RQ, ROWS)
+
+    def in_two(rows):
+        image_h[0:64, rows] = image_t[:, rows].astype(BF16)
+        image_h[64:128, rows] = (image_t[:, rows] - image_h[0:64, rows].astype(F32)).astype(BF16)
+
+    def project(rows, start, width):
+        p = dot(image_h[:, rows], merged[rows, at(start, width, 128)])
+        return p[0:64] + p[64:128]
+
+    def hand_over(side, rows):
+        p = project(rows, (1 - c) * HALF, HALF)
+        ranks = slice(64 * side, 64 * side + 64)
+        for n in range(3):
+            psend[n, ranks, :] = p[:, PART * n:PART * n + PART].astype(BF16)
+            send(psend.at[n, ranks], psib.at[n, ranks], s_p.at[side, n], r_p.at[side, n], device(dc=1))
+
+    lax.fori_loop(0, 2, finish, 0)
+    in_two(query)
+    hand_over(0, query)
+    qown[...] = project(query, c * HALF, HALF)
+    finish(2, 0)
+    in_two(key)
+    hand_over(1, key)
 
     def split(k):
         first, last = lax.div(2 - k, 2), lax.div(k, 2)
@@ -188,36 +202,49 @@
         first, middle, last = split(k)
         return z * (1 - last) + y * last, y * first + x * (1 - first), x * first + y * middle + z * last
 
-    def move(k, da, db):
+    def turned(v):
+        return [lax.rem(v + d, 4) for d in range(4)]
+
+    zs, ys, xs = turned(z), turned(y), turned(x)
+
+    def plane(k):
         first, middle, last = split(k)
-        return device(da * (1 - last), db * first + da * last, db * (1 - first))
+        far = range(4)
+        dp_a = [(4 * zs[d] + y * middle) * (1 - last) + (4 * z + ys[d]) * last for d in far]
+        dp_b = [ys[d] * first for d in far]
+        tensor_b = [2 * (x * first + xs[d] * (1 - first)) + c for d in far]
+        rows_a = [32 * (zs[d] * (1 - last) + ys[d] * last) for d in far]
+        b = [ys[d] * first + xs[d] * (1 - first) for d in far]
+        rows_b = [16 * lax.div(v, 2) for v in b]
+        lanes_b = [LANES * lax.rem(v, 2) for v in b]
+
+        def peer(da, db):
+            return dp_a[da] + dp_b[db], tensor_b[db]
+
+        def spot(da, db):
+            return at(rows_a[da] + rows_b[db], 16, 16), lanes_b[db]
+
+        return peer, spot
 
     def along(k, d):
         first, middle, last = split(k)
         return device(d * last, d * middle, d * first)
 
-    def slice_of(a, b):
-        return at(16 * (2 * a + lax.div(b, 2)), 16, 16), LANES * lax.rem(b, 2)
-
     around = [(da, db) for da in range(4) for db in range(4) if (da, db) != (0, 0)]
     around.sort(key=lambda o: -(min(o[0], 4 - o[0]) + min(o[1], 4 - o[1])))
 
-    q, kk = project((1 - c) * HALF, HALF)
-    for n in range(3):
-        psend[n, 0:64, :] = q[:, PART * n:PART * n + PART].astype(BF16)
-        psend[n, 64:128, :] = kk[:, PART * n:PART * n + PART].astype(BF16)
-        send(psend.at[n], psib.at[n], s_p.at[n], r_p.at[n], device(dc=1))
-
     def share(k, carry):
-        q, kk = project(c * HALF + PART * k)
-        arrived(psib.at[k], r_p.at[k], s_p.at[k])
-        pown[k, 0:64, :] = (q + psib[k, 0:64, :].astype(F32)).astype(BF16)
+        kk = project(key, c * HALF + PART * k, PART)
+        for side in (0, 1):
+            arrived(psib.at[k, 64 * side:64 * side + 64], r_p.at[side, k], s_p.at[side, k])
+        pown[k, 0:64, :] = (qown[:, at(PART * k, PART, 128)] + psib[k, 0:64, :].astype(F32)).astype(BF16)
         pown[k, 64:128, :] = (kk + psib[k, 64:128, :].astype(F32)).astype(BF16)
         a, b, _ = place(k)
+        peer, spot = plane(k)
         for da, db in around:
-            rows, lanes = slice_of(lax.rem(a + da, 4), lax.rem(b + db, 4))
-            send(pown.at[k, rows, at(lanes, LANES, 128)], rs.at[k, 4 * a + b], s_rs.at[k], r_rs.at[k], move(k, da, db))
-        rows, lanes = slice_of(a, b)
+            rows, lanes = spot(da, db)
+            send(pown.at[k, rows, at(lanes, LANES, 128)], rs.at[k, 4 * a + b], s_rs.at[k], r_rs.at[k], peer(da, db))
+        rows, lanes = spot(0, 0)
         rs[k, 4 * a + b] = pown[k, rows, at(lanes, LANES, 128)]
 
         return carry
@@ -251,12 +278,12 @@
         total = ar3[k, 0].astype(F32)
         for s in (1, 2, 3):
             total += ar3[k, s].astype(F32)
-        a, b, _ = place(k)
-        rows, lanes = slice_of(a, b)
-        spot = (rows, at(c * HALF + PART * k + lanes, LANES, 128))
-        psum[spot] = total.astype(BF16)
+        peer, spot = plane(k)
+        rows, lanes = spot(0, 0)
+        here = (rows, at(c * HALF + PART * k + lanes, LANES, 128))
+        psum[here] = total.astype(BF16)
         for da, db in around:
-            send(psum.at[spot], psum.at[spot], s_ag.at[k], r_ag.at[k], move(k, da, db))
+            send(psum.at[here], psum.at[here], s_ag.at[k], r_ag.at[k], peer(da, db))
         return carry
 
     lax.fori_loop(0, 3, spread, 0)
@@ -297,7 +324,8 @@
             sent(ar1.at[k, h, 0:3], r_ar1.at[k, h], s_ar1.at[k, h])
             sent(ar2.at[k, h, 0:3], r_ar2.at[k, h], s_ar2.at[k, h])
     for k in range(3):
-        sent(psend.at[k], r_p.at[k], s_p.at[k])
+        for side in (0, 1):
+            sent(psend.at[k, 64 * side:64 * side + 64], r_p.at[side, k], s_p.at[side, k])
         sent(rs.at[k, 0:15], r_rs.at[k], s_rs.at[k])
         sent(ar3.at[k, 0:3], r_a3.at[k], s_a3.at[k])
         sent(rs.at[k, 0:15], r_ag.at[k], s_ag.at[k])
@@ -331,6 +359,7 @@
             vmem((RANK, 128), F32),
             vmem((RANK, 128), F32),
             vmem((4, RANK, 128), F32),
+            vmem((RANK, HALF), F32),
             vmem((3, 128, PART), BF16),
             vmem((3, 128, PART), BF16),
             vmem((3, 128, PART), BF16),
@@ -339,7 +368,7 @@
             dma((BLOCKS,)), dma,
             dma((BLOCKS, 2)), dma((BLOCKS, 2)), dma((BLOCKS, 2)), dma((BLOCKS, 2)),
             dma, dma, dma, dma,
-            dma((3,)), dma((3,)), dma((3,)), dma((3,)), dma((3,)), dma((3,)),
+            dma((2, 3)), dma((2, 3)), dma((3,)), dma((3,)), dma((3,)), dma((3,)),
             dma((3,)), dma((3,)), dma((3,)), dma((3,)),
         ],
         compiler_params=pltpu.CompilerParams(

time: 45.3 us -> 45.1 us (level)
  no operation moved by 1% of the time
where the time goes in v5:
time: 45.1 us; the launch traced here: 45 us
  Pallas kernels  44.4 us (98%)
  between operations  0.64 us (1%)
    pallas_call x1, Pallas kernels, reduce(): pl.pallas_call(reduce_kernel, name='reduce', out_shape=(vmem((ROWS, D), B...  41 us
    pallas_call x1, Pallas kernels, refresh(): pl.pallas_call(refresh_kernel, name='refresh', out_shape=(jax.ShapeDtypeS...  3.34 us

profile of v5, /device:TPU:1, one launch (start us, length us, event | category | flops | bytes accessed | tf_op | source)
XLA Modules:
  0.0 45.0 jit_solution(5109249508378460027)
XLA Ops:
  0.6 41.0 %reduce.1 = (bf16[768,4608]{1,0:T(8,128)(2,1)S(1)}, bf16[768,64]{1,0:T(8,128)(2,1)S(1)}, bf16[128,4608]{1,0:T(8,128)(2,1)S(1)}) custom-call(bf16[1,1,512,4608]{3,2,1,0:T(8,128)(2,1)} %gq.1, bf16[1,1,256,4608]{3,2,1,0:T(8,128)(2,1)} %gk.1, bf16[1,1,512,4608]{3,2,1,0:T(8,128)(2,1)} %eq.1, bf16[1,1,256,4608]{3,2,1,0:T(8,128)(2,1)} %ek.1, ...), custom_call_target="tpu_custom_call" | custom-call | tf_op jit(solution)/shard_map/reduce/pallas_call | solution.py:339
  41.7 3.3 %refresh.1 = (bf16[1,1,512,4608]{3,2,1,0:T(8,128)(2,1)}, bf16[1,1,256,4608]{3,2,1,0:T(8,128)(2,1)}, bf16[1,64,4608]{2,1,0:T(8,128)(2,1)}, bf16[1,64,4608]{2,1,0:T(8,128)(2,1)}) custom-call(bf16[768,4608]{1,0:T(8,128)(2,1)S(1)} %get-tuple-element.11.merged, bf16[768,64]{1,0:T(8,128)(2,1)S(1)} %get-tuple-element.12.basis, ...), custom_call_target="tpu_custom_call" | custom-call | tf_op jit(solution)/shard_map/refresh/pallas_call | solution.py:413

commit v6 on v5

--- a/solution.py
+++ b/solution.py
@@ -203,7 +203,7 @@
         return z * (1 - last) + y * last, y * first + x * (1 - first), x * first + y * middle + z * last
 
     def turned(v):
-        return [lax.rem(v + d, 4) for d in range(4)]
+        return [lax.rem(v + d * (1 - 2 * c) + 4, 4) for d in range(4)]
 
     zs, ys, xs = turned(z), turned(y), turned(x)
 

time: 45.1 us -> 45.1 us (level)
  no operation moved by 1% of the time
where the time goes in v6:
time: 45.1 us; the launch traced here: 45 us
  Pallas kernels  44.4 us (98%)
  between operations  0.64 us (1%)
    pallas_call x1, Pallas kernels, reduce(): pl.pallas_call(reduce_kernel, name='reduce', out_shape=(vmem((ROWS, D), B...  41 us
    pallas_call x1, Pallas kernels, refresh(): pl.pallas_call(refresh_kernel, name='refresh', out_shape=(jax.ShapeDtypeS...  3.34 us

profile of v6, /device:TPU:1, one launch (start us, length us, event | category | flops | bytes accessed | tf_op | source)
XLA Modules:
  0.0 45.0 jit_solution(5107923278993110704)
XLA Ops:
  0.6 41.0 %reduce.1 = (bf16[768,4608]{1,0:T(8,128)(2,1)S(1)}, bf16[768,64]{1,0:T(8,128)(2,1)S(1)}, bf16[128,4608]{1,0:T(8,128)(2,1)S(1)}) custom-call(bf16[1,1,512,4608]{3,2,1,0:T(8,128)(2,1)} %gq.1, bf16[1,1,256,4608]{3,2,1,0:T(8,128)(2,1)} %gk.1, bf16[1,1,512,4608]{3,2,1,0:T(8,128)(2,1)} %eq.1, bf16[1,1,256,4608]{3,2,1,0:T(8,128)(2,1)} %ek.1, ...), custom_call_target="tpu_custom_call" | custom-call | tf_op jit(solution)/shard_map/reduce/pallas_call | solution.py:339
  41.7 3.3 %refresh.1 = (bf16[1,1,512,4608]{3,2,1,0:T(8,128)(2,1)}, bf16[1,1,256,4608]{3,2,1,0:T(8,128)(2,1)}, bf16[1,64,4608]{2,1,0:T(8,128)(2,1)}, bf16[1,64,4608]{2,1,0:T(8,128)(2,1)}) custom-call(bf16[768,4608]{1,0:T(8,128)(2,1)S(1)} %get-tuple-element.11.merged, bf16[768,64]{1,0:T(8,128)(2,1)S(1)} %get-tuple-element.12.basis, ...), custom_call_target="tpu_custom_call" | custom-call | tf_op jit(solution)/shard_map/refresh/pallas_call | solution.py:413
